TPU v7x, 256 devices: a whole 4x4x8 slice. The times are simulated.
256 devices in a mesh: gx: 8 (over x, core), gy: 4 (over y), gz: 8 (over z).
Axes of the slice: x: 4, y: 4, z: 8, core: 2. Of those that a mesh axis runs over, the one named last changes fastest.
Arguments:
- conserved: float32 [1024, 5, 4096], P(('gx', 'gy', 'gz')), as said below
- old_owner: int32 [512], replicated, may hold values from 0 to 255, as said below
- new_owner: int32 [512], replicated, may hold values from 0 to 255, as said below
- box_level: int32 [512], replicated, may hold values from 0 to 2
- face_source: int32 [1024, 6], P(('gx', 'gy', 'gz')), may hold values from 0 to 7, as said below
- coarse_part: int32 [1024, 6], P(('gx', 'gy', 'gz')), may hold values from 0 to 4
Outputs:
- new_state: float32 [768, 5, 4096], P(('gx', 'gy', 'gz'))
Inputs may be any that keep to these rules, and one draw needn't show every extreme that they name: Boxes are numbered along a Morton curve and old_owner never falls along the numbering. Every device owns 1 to 4 boxes before regridding, and some device owns exactly 4. `new_owner`: each box's new owner is its old owner or one of the two devices next to it in the device order. The boxes that a device passes to its lower neighbour are the first ones it owned, those it passes to its upper neighbour the last ones. At most 1 box crosses each boundary between consecutive devices in each direction; all boundaries but three carry exactly 1 in each direction. Every device owns 1 to 3 boxes after regridding, and some device owns exactly 3. For every occupied old slot, the slot that face_source names is occupied. Entries of empty slots also lie in the range. `conserved`: in every cell of every slot the density and the pressure 0.4 (energy - |momentum|^2 / (2 density)) lie between 0.3 and 3, and each velocity component between -1.5 and 1.5.
All inputs are finite; a program needn't handle non-finite values.
Results may differ from a plain program's by a relative error of at most 0.0003.
Values sent between devices are 32-bit elements; how exact they have to be, the bound alone decides.
No kernel may reach another device: no remote copies, remote signals or barrier semaphores. Data moves between devices by JAX's collectives and lax.ppermute only.
A program may use at most 128 MiB of HBM per device.

v0:
```python
import jax
import jax.numpy as jnp
from jax import lax
from jax.experimental import pallas as pl
from jax.experimental.pallas import tpu as pltpu
from jax.sharding import PartitionSpec as P

EDGE = 16
FIELDS = 5
LANES = 128
SUB = 8
SLOTS = 4
CELLS = FIELDS * EDGE
AXES = ("gx", "gy", "gz")
ORDER = ((0, 1, 2, 3, 4), (0, 2, 1, 3, 4), (0, 3, 1, 2, 4))
FACE_TILES = 12
INNER = 9
OUTER = 4
FACE_CHUNK = 3
PACKED = 2 * CELLS // SUB
VMEM_LIMIT = 48 * 1024 * 1024


def iota(axis):
    return lax.broadcasted_iota(jnp.int32, (SUB, LANES), axis)


def rows(tile, count=1):
    start = tile * SUB
    if not isinstance(start, int):
        start = pl.multiple_of(start, SUB)
    return pl.ds(start, count * SUB)


def get(ref, tile, count):
    return ref[rows(tile, count), :].reshape(count, SUB, LANES)


def put(ref, tile, value):
    count = value.shape[0]
    ref[rows(tile, count), :] = value.reshape(count * SUB, LANES)


def swap_bit(tiles, bit, axis, step):
    low = (iota(axis) & step) == 0
    across = iota(axis) ^ step
    out = list(tiles)
    for i in range(len(tiles)):
        if i & bit:
            continue
        j = i | bit
        a, b = tiles[i], tiles[j]
        moving = jnp.where(low, b, a)
        if 2 * step == (SUB, LANES)[axis]:
            moved = pltpu.roll(moving, step, axis)
        else:
            moved = jnp.take_along_axis(moving, across, axis=axis)
        out[i] = jnp.where(low, a, moved)
        out[j] = jnp.where(low, moved, b)
    return out


def swap_xy(tiles):
    tiles = swap_bit(tiles, 8, 0, 4)
    for bit, step in ((4, 64), (2, 32), (1, 16)):
        tiles = swap_bit(tiles, bit, 1, step)
    return tiles


def z_tile(ref, field, z):
    return ref[pl.ds(field * EDGE * SUB + z, SUB, stride=EDGE), :]


def from_z(tiles, turn_ref):
    for z in range(EDGE):
        turn_ref[pl.ds(z, SUB, stride=EDGE), :] = tiles[z]
    whole = turn_ref[...].T
    return [whole[k * SUB : (k + 1) * SUB] for k in range(EDGE)]


def primitives(rho, mx, my, mz, energy):
    inv = 1.0 / rho
    u, v, w = mx * inv, my * inv, mz * inv
    p = 0.4 * (energy - 0.5 * rho * (u * u + v * v + w * w))
    return rho, u, v, w, p


def face_tile(field):
    return 2 * field


def is_even(axis):
    return lax.rem(lax.axis_index(axis), 2) == 0


def layers_kernel(c_ref, *refs):
    near, far = refs[0:3], refs[3:6]
    w_ref, z_ref = refs[6:8]
    even = [is_even(axis) for axis in AXES]
    for x in range(EDGE):
        got = [c_ref[rows(f * EDGE + x), :] for f in range(FIELDS)]
        for f, value in enumerate(primitives(*got)):
            w_ref[rows(f * EDGE + x), :] = value
    for f in range(FIELDS):
        depth = 4 if f == 4 else 2
        tiles = [w_ref[rows(f * EDGE + x), :] for x in range(EDGE)]
        z_ref[rows(f * EDGE, EDGE), :] = w_ref[rows(f * EDGE, EDGE), :].T
        turned_z = [z_tile(z_ref, f, z) for z in range(EDGE)]
        turned = (tiles, swap_xy(tiles), turned_z)
        for axis in range(3):
            for r in range(depth):
                low, high = turned[axis][r], turned[axis][EDGE - depth + r]
                place = rows(face_tile(f) + r)
                near[axis][place, :] = jnp.where(even[axis], high, low)
                far[axis][place, :] = jnp.where(even[axis], low, high)


def device_position():
    place = lax.axis_index(AXES[0])
    for axis in AXES[1:]:
        place = place * lax.axis_size(axis) + lax.axis_index(axis)
    return place


def find_boxes(old_ref, new_ref):
    boxes = old_ref.shape[0]
    place = device_position()

    def halve(_, ends):
        low, high = ends
        middle = (low + high) // 2
        below = old_ref[jnp.minimum(middle, boxes - 1)] < place
        open_ends = low < high
        return (
            jnp.where(open_ends & below, middle + 1, low),
            jnp.where(open_ends & jnp.logical_not(below), middle, high),
        )

    ends = (jnp.int32(0), jnp.int32(boxes))
    for step in range(boxes.bit_length()):
        ends = halve(step, ends)
    low = ends[0]
    count = jnp.int32(0)
    for k in range(SLOTS):
        at = low + k
        mine = (at < boxes) & (old_ref[jnp.minimum(at, boxes - 1)] == place)
        count = count + mine.astype(jnp.int32)
    high = low + count
    before = jnp.maximum(low - 1, 0)
    after = jnp.minimum(high, boxes - 1)
    up_in = ((low > 0) & (new_ref[before] == place)).astype(jnp.int32)
    down_in = ((high < boxes) & (new_ref[after] == place)).astype(jnp.int32)
    down_out = (new_ref[low] == place - 1).astype(jnp.int32)
    up_out = (new_ref[high - 1] == place + 1).astype(jnp.int32)
    return low, count, up_in, down_in, down_out, up_out


def by_slot(values, axis=0):
    slot = iota(axis) & 3
    out = jnp.full((SUB, LANES), values[0])
    for b in range(1, SLOTS):
        out = jnp.where(slot == b, values[b], out)
    return out


def limited(p, fields):
    n = p.shape[0] - 6
    jump = jnp.abs(p[3 : n + 5] - p[1 : n + 3])
    flat = jnp.clip(1.0 - 2.0 * jump / (p[4 : n + 6] + p[0 : n + 2]), 0.0, 1.0)
    weight = 0.5 * jnp.minimum(jnp.minimum(flat[0:n], flat[1 : n + 1]), flat[2 : n + 2])
    left, right = [], []
    for w in fields:
        diff = w[1 : n + 2] - w[0 : n + 1]
        back, ahead = diff[0:n], diff[1 : n + 1]
        mean = 0.5 * (back + ahead)
        twice = diff + diff
        back2, ahead2 = twice[0:n], twice[1 : n + 1]
        rise = jnp.maximum(jnp.minimum(mean, jnp.minimum(back2, ahead2)), 0.0)
        fall = jnp.minimum(jnp.maximum(mean, jnp.maximum(back2, ahead2)), 0.0)
        shift = weight * (rise + fall)
        left.append(w[1 : n + 1] + shift)
        right.append(w[1 : n + 1] - shift)
    return left, right


def hllc(left, right):
    rho_l, u_l, v_l, w_l, p_l = left
    rho_r, u_r, v_r, w_r, p_r = right
    ratio_l = p_l / rho_l
    ratio_r = p_r / rho_r
    c_l = jnp.sqrt(1.4 * ratio_l)
    c_r = jnp.sqrt(1.4 * ratio_r)
    s_l = jnp.minimum(u_l - c_l, u_r - c_r)
    s_r = jnp.maximum(u_l + c_l, u_r + c_r)
    m_l = rho_l * (s_l - u_l)
    m_r = rho_r * (s_r - u_r)
    mid = (p_r - p_l + m_l * u_l - m_r * u_r) / (m_l - m_r)
    use_left = (s_l >= 0.0) | (mid >= 0.0)

    def pick(a, b):
        return jnp.where(use_left, a, b)

    rho, u, v, w, p = (
        pick(rho_l, rho_r),
        pick(u_l, u_r),
        pick(v_l, v_r),
        pick(w_l, w_r),
        pick(p_l, p_r),
    )
    ratio, mass = pick(ratio_l, ratio_r), pick(m_l, m_r)
    wave = pick(jnp.minimum(s_l, 0.0), jnp.maximum(s_r, 0.0))
    starred = wave != 0.0
    scale = jnp.where(starred, wave / jnp.where(starred, wave - mid, 1.0), 0.0)
    f_mass = rho * (u - wave) + scale * mass
    push = scale * (mid - u)
    energy = 2.5 * ratio + 0.5 * (u * u + v * v + w * w)
    return (
        f_mass,
        u * f_mass + push * mass + p,
        v * f_mass,
        w * f_mass,
        energy * f_mass + p * u + push * (mid * mass + p),
    )


def field_line(x_ref, y_ref, z_ref, axis, place, start, stop):
    field = ORDER[axis][place]
    if axis == 2:
        return jnp.stack([z_tile(z_ref, field, z) for z in range(start, stop)])
    return get(y_ref if axis else x_ref, field * EDGE + start, stop - start)


def inner_kernel(*refs):
    far = refs[0:5]
    w_ref, z_ref = refs[5:7]
    info_ref, index_ref, scale_ref, y_ref, flux_ref, edge_ref = refs[7:13]
    left_ref, right_ref = refs[13:15]
    old_ref, new_ref, level_ref, source_ref, coarse_ref = here = refs[15:20]
    sems = refs[20]
    copies = [pltpu.make_async_copy(a, b, sems.at[k]) for k, (a, b) in enumerate(zip(far, here))]
    for copy in copies:
        copy.start()

    for f in range(FIELDS):
        tiles = [w_ref[rows(f * EDGE + x), :] for x in range(EDGE)]
        for k, value in enumerate(swap_xy(tiles)):
            y_ref[rows(f * EDGE + k), :] = value
    for axis in range(3):
        lines = (w_ref, y_ref, z_ref, axis)
        p = field_line(*lines, 4, 0, EDGE)
        fields = [field_line(*lines, k, 2, INNER + 5) for k in range(FIELDS)]
        left, right = limited(p, fields)
        for k in range(FIELDS):
            put(left_ref, (k * 3 + axis) * INNER, left[k][0:INNER])
            put(right_ref, (k * 3 + axis) * INNER, right[k][1 : INNER + 1])
            put(edge_ref, (axis * 2) * FIELDS + k, right[k][0:1])
            put(edge_ref, (axis * 2 + 1) * FIELDS + k, left[k][INNER : INNER + 1])
    for copy in copies:
        copy.wait()
    low, count, up_in, down_in, down_out, up_out = find_boxes(old_ref, new_ref)
    boxes = old_ref.shape[0]
    staying = count - down_out - up_out
    info_ref[0] = count - 1
    slot = iota(0) & 3
    lower = jnp.where(is_even(AXES[-1]), 3, 2)
    taken = up_in + staying
    code = jnp.where(slot < taken, 1, jnp.where(slot < taken + down_in, 5 - lower, 0))
    index_ref[rows(18), :] = jnp.where(slot < up_in, lower, code)
    index_ref[rows(19), :] = (iota(0) & 4) + ((slot + down_out - up_in) & 3)
    steps = []
    for b in range(SLOTS):
        level = level_ref[jnp.minimum(low + b, boxes - 1)]
        steps.append(
            jnp.where(level == 0, 0.02, jnp.where(level == 1, 0.04, 0.08)).astype(jnp.float32)
        )
    scale_ref[...] = by_slot(steps)
    sub, lane = iota(0), iota(1)
    for face in range(6):
        along = 1 if face // 2 == 2 else 0
        source = by_slot([source_ref[b, face] for b in range(SLOTS)], along)
        codes = by_slot([coarse_ref[b, face] for b in range(SLOTS)], along)
        is_coarse = codes > 0
        quadrant = codes - 1
        first, second = (quadrant >> 1) & 1, quadrant & 1
        if along == 0:
            half = sub >> 2
            from_row = (source & 3) + 4 * jnp.where(is_coarse, first, half)
            near = (half * 4 + (lane >> 5)) * EDGE + second * 8 + ((lane & 15) >> 1)
            from_lane = jnp.where(is_coarse, near, lane)
        else:
            half = (lane >> 2) & 1
            from_row = jnp.where(is_coarse, half * 4 + (sub >> 1), sub)
            near = (first * 8 + (lane >> 4)) * 8 + second * 4
            from_lane = (source & 3) + jnp.where(is_coarse, near, lane & 124)
        index_ref[rows(3 * face), :] = from_row
        index_ref[rows(3 * face + 1), :] = from_lane
        index_ref[rows(3 * face + 2), :] = (source >> 2) + 2 * is_coarse.astype(jnp.int32)

    for step in range(3 * INNER // FACE_CHUNK):

        def load(ref):
            return [get(ref, k * 3 * INNER + step * FACE_CHUNK, FACE_CHUNK) for k in range(FIELDS)]

        for k, value in enumerate(hllc(load(left_ref), load(right_ref))):
            put(flux_ref, k * 3 * INNER + step * FACE_CHUNK, value)


def outer_kernel(*refs):
    sent_info_ref, c_ref = refs[0:2]
    near_got, far_got = refs[2:5], refs[5:8]
    w_ref, z_ref, index_ref, scale_ref, y_ref, inner_ref, edge_ref = refs[8:15]
    new_ref, near_ref, far_ref = refs[15:18]
    ghost_ref, flux_ref, turn_ref, info_ref, sem = refs[18:23]
    even = [is_even(axis) for axis in AXES]
    copy = pltpu.make_async_copy(sent_info_ref, info_ref, sem)
    copy.start()

    for face in range(6):
        axis, side = face // 2, face % 2
        from_row = index_ref[rows(3 * face), :]
        from_lane = index_ref[rows(3 * face + 1), :]
        flags = index_ref[rows(3 * face + 2), :]
        is_own = (flags & 1) == 1
        is_coarse = flags >= 2
        use_near = even[axis] if side == 1 else jnp.logical_not(even[axis])
        turns = ((from_row, 0), (from_lane, 1))
        before, after = turns if axis < 2 else turns[::-1]
        for f in range(FIELDS):
            depth = 4 if f == 4 else 2
            picked = []
            start = EDGE - depth if side == 0 else 0
            layer = (ORDER[axis].index(f), start, start + depth)
            own = field_line(w_ref, y_ref, z_ref, axis, *layer)
            for r in range(depth):
                place = rows(face_tile(f) + r)
                theirs = jnp.where(
                    use_near, near_got[axis][place, :], far_got[axis][place, :]
                )
                picked.append(
                    jnp.where(
                        is_own,
                        jnp.take_along_axis(own[r], before[0], axis=before[1]),
                        jnp.take_along_axis(theirs, before[0], axis=before[1]),
                    )
                )
            for k in range(depth):
                source = picked[(depth // 2 if side == 0 else 0) + k // 2]
                chosen = jnp.where(is_coarse, source, picked[k])
                row = face * FACE_TILES + face_tile(ORDER[axis].index(f)) + k
                ghost_ref[rows(row), :] = jnp.take_along_axis(chosen, after[0], axis=after[1])

    for axis in range(3):
        for side in range(2):
            face = axis * 2 + side

            def line(k):
                depth = 4 if k == 4 else 2
                ghost = get(ghost_ref, face * FACE_TILES + face_tile(k), depth)
                near = (0, depth + 2) if side == 0 else (EDGE - depth - 2, EDGE)
                near = field_line(w_ref, y_ref, z_ref, axis, k, *near)
                return jnp.concatenate((ghost, near) if side == 0 else (near, ghost), axis=0)

            p = line(4)
            fields = [line(k) for k in range(4)] + [p[2:8]]
            left, right = limited(p, fields)
            edge = [get(edge_ref, face * FIELDS + k, 1) for k in range(FIELDS)]
            if side == 0:
                right = [jnp.concatenate([a[1:], b], axis=0) for a, b in zip(right, edge)]
            else:
                left = [jnp.concatenate([b, a[:-1]], axis=0) for a, b in zip(left, edge)]
            for k, value in enumerate(hllc(left, right)):
                put(flux_ref, (face * FIELDS + k) * OUTER, value)

    def change(axis, field):
        place = ORDER[axis].index(field)
        faces = [
            flux_ref[rows((axis * 2 * FIELDS + place) * OUTER + k), :] for k in range(OUTER)
        ]
        faces += [inner_ref[rows((place * 3 + axis) * INNER + k), :] for k in range(INNER)]
        faces += [
            flux_ref[rows(((axis * 2 + 1) * FIELDS + place) * OUTER + k), :] for k in range(OUTER)
        ]
        return [faces[k + 1] - faces[k] for k in range(EDGE)]

    scale = scale_ref[...]
    for f in range(FIELDS):
        along_x = change(0, f)
        along_y = swap_xy(change(1, f))
        along_z = from_z(change(2, f), turn_ref.at[rows(f * EDGE, EDGE)])
        for x in range(EDGE):
            total = along_x[x] + along_y[x] + along_z[x]
            place = rows(f * EDGE + x)
            new_ref[place, :] = c_ref[place, :] - scale * total
    copy.wait()
    last = info_ref[0]
    up_near = even[2].astype(jnp.int32)
    for slot, out in ((last * up_near, near_ref), (last * (1 - up_near), far_ref)):
        for t in range(2):
            for n in range(CELLS // SUB):
                out[rows(t * (CELLS // SUB) + n), :] = new_ref[
                    pl.ds(n * 64 + 4 * t + slot, SUB, stride=SUB), :
                ]


def settle_kernel(index_ref, new_ref, out_ref):
    stays = index_ref[rows(18), :] == 1
    from_row = index_ref[rows(19), :]
    for n in range(CELLS):
        value = jnp.take_along_axis(new_ref[rows(n), :], from_row, axis=0)
        out_ref[rows(n), :] = jnp.where(stays, value, 0.0)


def place_kernel(index_ref, settled_ref, near_ref, far_ref, out_ref, ready_ref, sems):
    code = index_ref[rows(18), :]
    first = iota(0) < 4
    from_near, from_far = code == 2, code == 3
    copies = []
    for f in range(FIELDS):
        for x in range(EDGE):
            n = f * EDGE + x

            def spread(ref):
                a = jnp.broadcast_to(ref[pl.ds(n, 1), :], (SUB, LANES))
                b = jnp.broadcast_to(ref[pl.ds(CELLS + n, 1), :], (SUB, LANES))
                return jnp.where(first, a, b)

            value = settled_ref[rows(n), :]
            value = jnp.where(from_near, spread(near_ref), value)
            value = jnp.where(from_far, spread(far_ref), value)
            for t in range(2):
                lanes = slice((2 * x + t) * LANES, (2 * x + t + 1) * LANES)
                ready_ref[f, :, lanes] = value[4 * t : 4 * t + 3]
        copies.append(pltpu.make_async_copy(ready_ref.at[f], out_ref.at[f], sems.at[f]))
        copies[-1].start()
    for copy in copies:
        copy.wait()


def swap_with(value, axis, first):
    count = 1
    for name in (axis,) if isinstance(axis, str) else axis:
        count *= lax.axis_size(name)
    pairs = [(k, (k + 1) % count) for k in range(first, count, 2)]
    return lax.ppermute(value, axis, pairs + [(b, a) for a, b in pairs])


def tiles_of(count, dtype=jnp.float32):
    return jax.ShapeDtypeStruct((count * SUB, LANES), dtype)


def scratch(count):
    return pltpu.VMEM((count * SUB, LANES), jnp.float32)


def local(conserved, old_owner, new_owner, box_level, face_source, coarse_part):
    vmem = pl.BlockSpec(memory_space=pltpu.VMEM)
    smem = pl.BlockSpec(memory_space=pltpu.SMEM)
    hbm = pl.BlockSpec(memory_space=pltpu.HBM)
    params = pltpu.CompilerParams(vmem_limit_bytes=VMEM_LIMIT)
    cells = conserved.transpose(1, 0, 2).reshape(FIELDS, SLOTS, 2 * EDGE, LANES)
    cells = cells.transpose(0, 2, 1, 3).reshape(CELLS * SUB, LANES)
    *sent, along_x, along_z = pl.pallas_call(
        layers_kernel,
        out_shape=[tiles_of(FACE_TILES)] * 6 + [tiles_of(CELLS)] * 2,
        in_specs=[vmem],
        out_specs=[vmem] * 8,
        compiler_params=params,
        name="layers",
    )(cells)
    got = [swap_with(sent[k], AXES[k % 3], k // 3) for k in range(6)]
    small = (old_owner, new_owner, box_level, face_source, coarse_part)
    info, index, *inner = pl.pallas_call(
        inner_kernel,
        out_shape=[
            jax.ShapeDtypeStruct((8,), jnp.int32),
            tiles_of(20, jnp.int32),
            tiles_of(1),
            tiles_of(CELLS),
            tiles_of(FIELDS * 3 * INNER),
            tiles_of(6 * FIELDS),
        ],
        in_specs=[hbm] * 5 + [vmem] * 2,
        out_specs=[smem] + [vmem] * 5,
        scratch_shapes=[scratch(FIELDS * 3 * INNER)] * 2
        + [pltpu.SMEM(value.shape, jnp.int32) for value in small]
        + [pltpu.SemaphoreType.DMA((5,))],
        compiler_params=params,
        name="inner",
    )(*small, along_x, along_z)
    updated, near, far = pl.pallas_call(
        outer_kernel,
        out_shape=[tiles_of(CELLS), tiles_of(PACKED), tiles_of(PACKED)],
        in_specs=[pl.BlockSpec(memory_space=pl.ANY)] + [vmem] * 14,
        out_specs=[vmem] * 3,
        scratch_shapes=[
            scratch(6 * FACE_TILES),
            scratch(6 * FIELDS * OUTER),
            scratch(CELLS),
            pltpu.SMEM((8,), jnp.int32),
            pltpu.SemaphoreType.DMA(()),
        ],
        compiler_params=params,
        name="outer",
    )(
        info,
        cells,
        *got,
        along_x,
        along_z,
        index,
        *inner,
    )
    from_far = swap_with(far, AXES, 1)
    from_near = swap_with(near, AXES, 0)
    settled = pl.pallas_call(
        settle_kernel,
        out_shape=tiles_of(CELLS),
        in_specs=[vmem] * 2,
        out_specs=vmem,
        compiler_params=params,
        name="settle",
    )(index, updated)
    out_shape = (FIELDS, 3, EDGE**3)
    out = pl.pallas_call(
        place_kernel,
        out_shape=jax.ShapeDtypeStruct(out_shape, jnp.float32),
        in_specs=[vmem] * 4,
        out_specs=hbm,
        scratch_shapes=[
            pltpu.VMEM(out_shape, jnp.float32),
            pltpu.SemaphoreType.DMA((FIELDS,)),
        ],
        compiler_params=params,
        name="place",
    )(index, settled, from_near, from_far)
    return out.transpose(1, 0, 2)


def solution(mesh):
    return jax.shard_map(
        local,
        mesh=mesh,
        in_specs=(P(AXES, None, None), P(), P(), P(), P(AXES, None), P(AXES, None)),
        out_specs=P(AXES, None, None),
        check_vma=False,
    )
```

profile of v0, /device:TPU:1, one launch (start us, length us, event | category | flops | bytes accessed | tf_op | source)
XLA Modules:
  0.0 26.4 jit_solution(11643187546522829762)
XLA Ops:
  0.0 0.0 copy-start
  0.0 1.0 %copy-done = f32[4,5,4096]{2,0,1:T(4,128)S(1)} copy-done((f32[4,5,4096]{2,0,1:T(4,128)S(1)}, f32[4,5,4096]{2,0,1:T(4,128)}, u32[]{:S(2)}) %copy-start) | copy-done | bytes 327704
  1.0 0.5 %layers.1 = (f32[96,128]{1,0:T(8,128)S(1)}, f32[96,128]{1,0:T(8,128)S(1)}, f32[96,128]{1,0:T(8,128)S(1)}, f32[96,128]{1,0:T(8,128)S(1)}, f32[96,128]{1,0:T(8,128...) custom-call(f32[640,128]{1,0:T(8,128)S(1)} %bitcast.8), custom_call_target="tpu_custom_call" | custom-call | tf_op jit(solution)/shard_map/layers/pallas_call | solution.py:462
  1.5 3.3 %collective-permute-start = (f32[96,128]{1,0:T(8,128)S(1)}, f32[96,128]{1,0:T(8,128)S(1)}, u32[]{:S(2)}, u32[]{:S(2)}) collective-permute-start(f32[96,128]{1,0:T(8,128)S(1)} %get-tuple-element.26), channel_id=1, source_target_pairs={{0,32},{64,96},{128,160},{192,224},{32,0},{96,64},{160,128},{224,1... | collective-permute-start | bytes 147464 | tf_op jit(solution)/shard_map/ppermute | solution.py:444
  4.8 0.0 copy-start.6
  4.8 0.0 collective-permute-start.1
  4.8 1.2 %collective-permute-start.2 = (f32[96,128]{1,0:T(8,128)S(1)}, f32[96,128]{1,0:T(8,128)S(1)}, u32[]{:S(2)}, u32[]{:S(2)}) collective-permute-start(f32[96,128]{1,0:T(8,128)S(1)} %get-tuple-element.28), channel_id=1, source_target_pairs={{0,1},{2,3},{4,5},{6,7},{1,0},{3,2},{5,4},{7,6},{8,9},{10,11},{12,... | collective-permute-start | bytes 147464 | tf_op jit(solution)/shard_map/ppermute | solution.py:444
  6.0 0.0 copy-start.4
  6.0 0.0 copy-start.5
  6.0 1.7 %collective-permute-start.3 = (f32[96,128]{1,0:T(8,128)S(1)}, f32[96,128]{1,0:T(8,128)S(1)}, u32[]{:S(2)}, u32[]{:S(2)}) collective-permute-start(f32[96,128]{1,0:T(8,128)S(1)} %get-tuple-element.29), channel_id=1, source_target_pairs={{32,64},{96,128},{160,192},{224,0},{64,32},{128,96},{192,160},{0,2... | collective-permute-start | bytes 147464 | tf_op jit(solution)/shard_map/ppermute | solution.py:444
  7.8 1.9 %collective-permute-start.4 = (f32[96,128]{1,0:T(8,128)S(1)}, f32[96,128]{1,0:T(8,128)S(1)}, u32[]{:S(2)}, u32[]{:S(2)}) collective-permute-start(f32[96,128]{1,0:T(8,128)S(1)} %get-tuple-element.30), channel_id=1, source_target_pairs={{8,16},{24,0},{16,8},{0,24},{9,17},{25,1},{17,9},{1,25},{10,18},{2... | collective-permute-start | bytes 147464 | tf_op jit(solution)/shard_map/ppermute | solution.py:444
  9.7 0.0 collective-permute-done.refs_2_
  9.7 0.0 copy-start.3
  9.7 0.0 copy-start.2
  9.7 4.7 %collective-permute-start.5 = (f32[96,128]{1,0:T(8,128)S(1)}, f32[96,128]{1,0:T(8,128)S(1)}, u32[]{:S(2)}, u32[]{:S(2)}) collective-permute-start(f32[96,128]{1,0:T(8,128)S(1)} %get-tuple-element.31), channel_id=1, source_target_pairs={{1,2},{3,4},{5,6},{7,0},{2,1},{4,3},{6,5},{0,7},{9,10},{11,12},{13... | collective-permute-start | bytes 147464 | tf_op jit(solution)/shard_map/ppermute | solution.py:444
  14.4 0.0 copy-done.6
  14.4 0.0 copy-done.4
  14.4 0.0 copy-done.5
  14.4 0.0 copy-done.3
  14.4 0.0 copy-done.2
  14.4 0.0 copy-start.1
  14.4 1.5 %inner.1 = (s32[8]{0:T(128)S(1)}, s32[160,128]{1,0:T(8,128)S(1)}, f32[8,128]{1,0:T(8,128)S(1)}, f32[640,128]{1,0:T(8,128)S(1)}, f32[1080,128]{1,0:T(8,128)S(1)}, /*index=5*/f32[240,128]{1,0:T(8,128)S(1)}) custom-call(s32[512]{0:T(512)S(1)} %copy-done.2, s32[512]{0:T(512)S(1)} %copy-done.3, s32[512]{0:T(512)S(1)} %copy-done.4, s32[4,6]{1,0:T(4,128)S(1)} %copy-done.5, ...), custom_call_target="tpu_custom_call" | custom-call | tf_op jit(solution)/shard_map/inner/pallas_call | solution.py:472
  15.9 0.0 collective-permute-done.1.refs_3_
  15.9 0.0 collective-permute-done.2.refs_4_
  15.9 0.0 collective-permute-done.3.refs_5_
  15.9 0.0 collective-permute-done.4.refs_6_
  16.0 0.0 collective-permute-done.5.refs_7_
  16.0 0.0 copy-done.1
  16.0 1.2 %outer.1 = (f32[640,128]{1,0:T(8,128)S(1)}, f32[160,128]{1,0:T(8,128)S(1)}, f32[160,128]{1,0:T(8,128)S(1)}) custom-call(s32[8]{0:T(128)S(1)} %get-tuple-element.25.refs_0_, f32[640,128]{1,0:T(8,128)S(1)} %bitcast.9, f32[96,128]{1,0:T(8,128)S(1)} %collective-permute-done.refs_2_, f32[96,128]{1,0:T(8,128)S(1)} %collective-permute-done.1.refs_3_, ...), custom_call_target="tpu_custom_call" | custom-call | tf_op jit(solution)/shard_map/outer/pallas_call | solution.py:490
  17.2 0.1 collective-permute-start.6
  17.3 5.6 %collective-permute-start.7 = (f32[160,128]{1,0:T(8,128)S(1)}, f32[160,128]{1,0:T(8,128)S(1)}, u32[]{:S(2)}, u32[]{:S(2)}) collective-permute-start(f32[160,128]{1,0:T(8,128)S(1)} %get-tuple-element.38), channel_id=1, source_target_pairs={{1,2},{3,4},{5,6},{7,8},{9,10},{11,12},{13,14},{15,16},{17,18},{19... | collective-permute-start | bytes 245768 | tf_op jit(solution)/shard_map/ppermute | solution.py:444
  22.9 0.0 collective-permute-done.6.near_ref
  22.9 2.7 %collective-permute-done.7.far_ref = f32[160,128]{1,0:T(8,128)S(1)} collective-permute-done((f32[160,128]{1,0:T(8,128)S(1)}, f32[160,128]{1,0:T(8,128)S(1)}, u32[]{:S(2)}, u32[]{:S(2)}) %collective-permute-start.7) | collective-permute-done | bytes 81952 | tf_op jit(solution)/shard_map/ppermute | solution.py:444
  25.6 0.8 %place.1 = f32[5,3,4096]{2,1,0:T(4,128)} custom-call(s32[160,128]{1,0:T(8,128)S(1)} %get-tuple-element.24.refs_10_.index_ref, f32[640,128]{1,0:T(8,128)S(1)} %settle.1.settled_ref, f32[160,128]{1,0:T(8,128)S(1)} %collective-permute-done.6.near_ref, f32[160,128]{1,0:T(8,128)S(1)} %collective-permute-done.7.far_ref), custom_call_target="tpu_custom_call" | custom-call | tf_op jit(solution)/shard_map/place/pallas_call | solution.py:524
  (1 shorter events, 0.0 us)
Async XLA Ops:
  0.0 1.0 %copy-start = (f32[4,5,4096]{2,0,1:T(4,128)S(1)}, f32[4,5,4096]{2,0,1:T(4,128)}, u32[]{:S(2)}) copy-start(f32[4,5,4096]{2,0,1:T(4,128)} %param.6) | copy-start | bytes 983044
  1.5 8.2 %collective-permute-start = (f32[96,128]{1,0:T(8,128)S(1)}, f32[96,128]{1,0:T(8,128)S(1)}, u32[]{:S(2)}, u32[]{:S(2)}) collective-permute-start(f32[96,128]{1,0:T(8,128)S(1)} %get-tuple-element.26), channel_id=1, source_target_pairs={{0,32},{64,96},{128,160},{192,224},{32,0},{96,64},{160,128},{224,1... | collective-permute-start | bytes 147464 | tf_op jit(solution)/shard_map/ppermute | solution.py:444
  4.8 9.6 %copy-start.6 = (s32[4,6]{1,0:T(4,128)S(1)}, s32[4,6]{1,0:T(4,128)}, u32[]{:S(2)}) copy-start(s32[4,6]{1,0:T(4,128)} %refs_4_.1) | copy-start | bytes 292
  4.8 11.1 %collective-permute-start.1 = (f32[96,128]{1,0:T(8,128)S(1)}, f32[96,128]{1,0:T(8,128)S(1)}, u32[]{:S(2)}, u32[]{:S(2)}) collective-permute-start(f32[96,128]{1,0:T(8,128)S(1)} %get-tuple-element.27), channel_id=1, source_target_pairs={{0,8},{16,24},{8,0},{24,16},{1,9},{17,25},{9,1},{25,17},{2,10},{18... | collective-permute-start | bytes 147464 | tf_op jit(solution)/shard_map/ppermute | solution.py:444
  4.8 11.1 %collective-permute-start.2 = (f32[96,128]{1,0:T(8,128)S(1)}, f32[96,128]{1,0:T(8,128)S(1)}, u32[]{:S(2)}, u32[]{:S(2)}) collective-permute-start(f32[96,128]{1,0:T(8,128)S(1)} %get-tuple-element.28), channel_id=1, source_target_pairs={{0,1},{2,3},{4,5},{6,7},{1,0},{3,2},{5,4},{7,6},{8,9},{10,11},{12,... | collective-permute-start | bytes 147464 | tf_op jit(solution)/shard_map/ppermute | solution.py:444
  6.0 8.3 %copy-start.4 = (s32[512]{0:T(512)S(1)}, s32[512]{0:T(512)}, u32[]{:S(2)}) copy-start(s32[512]{0:T(512)} %refs_2_.1) | copy-start | bytes 6148
  6.0 8.3 %copy-start.5 = (s32[4,6]{1,0:T(4,128)S(1)}, s32[4,6]{1,0:T(4,128)}, u32[]{:S(2)}) copy-start(s32[4,6]{1,0:T(4,128)} %refs_3_.1) | copy-start | bytes 292
  6.0 9.9 %collective-permute-start.3 = (f32[96,128]{1,0:T(8,128)S(1)}, f32[96,128]{1,0:T(8,128)S(1)}, u32[]{:S(2)}, u32[]{:S(2)}) collective-permute-start(f32[96,128]{1,0:T(8,128)S(1)} %get-tuple-element.29), channel_id=1, source_target_pairs={{32,64},{96,128},{160,192},{224,0},{64,32},{128,96},{192,160},{0,2... | collective-permute-start | bytes 147464 | tf_op jit(solution)/shard_map/ppermute | solution.py:444
  7.8 8.2 %collective-permute-start.4 = (f32[96,128]{1,0:T(8,128)S(1)}, f32[96,128]{1,0:T(8,128)S(1)}, u32[]{:S(2)}, u32[]{:S(2)}) collective-permute-start(f32[96,128]{1,0:T(8,128)S(1)} %get-tuple-element.30), channel_id=1, source_target_pairs={{8,16},{24,0},{16,8},{0,24},{9,17},{25,1},{17,9},{1,25},{10,18},{2... | collective-permute-start | bytes 147464 | tf_op jit(solution)/shard_map/ppermute | solution.py:444
  9.7 4.7 %copy-start.3 = (s32[512]{0:T(512)S(1)}, s32[512]{0:T(512)}, u32[]{:S(2)}) copy-start(s32[512]{0:T(512)} %refs_1_.1) | copy-start | bytes 6148
  9.7 4.7 %copy-start.2 = (s32[512]{0:T(512)S(1)}, s32[512]{0:T(512)}, u32[]{:S(2)}) copy-start(s32[512]{0:T(512)} %refs_0_.1) | copy-start | bytes 6148
  9.7 6.3 %collective-permute-start.5 = (f32[96,128]{1,0:T(8,128)S(1)}, f32[96,128]{1,0:T(8,128)S(1)}, u32[]{:S(2)}, u32[]{:S(2)}) collective-permute-start(f32[96,128]{1,0:T(8,128)S(1)} %get-tuple-element.31), channel_id=1, source_target_pairs={{1,2},{3,4},{5,6},{7,0},{2,1},{4,3},{6,5},{0,7},{9,10},{11,12},{13... | collective-permute-start | bytes 147464 | tf_op jit(solution)/shard_map/ppermute | solution.py:444
  14.4 1.6 %copy-start.1 = (f32[4,5,4096]{2,0,1:T(4,128)S(1)}, f32[4,5,4096]{2,0,1:T(4,128)}, u32[]{:S(2)}) copy-start(f32[4,5,4096]{2,0,1:T(4,128)} %param.6) | copy-start | bytes 983044
  17.2 5.7 %collective-permute-start.6 = (f32[160,128]{1,0:T(8,128)S(1)}, f32[160,128]{1,0:T(8,128)S(1)}, u32[]{:S(2)}, u32[]{:S(2)}) collective-permute-start(f32[160,128]{1,0:T(8,128)S(1)} %get-tuple-element.37), channel_id=1, source_target_pairs={{0,1},{2,3},{4,5},{6,7},{8,9},{10,11},{12,13},{14,15},{16,17},{18,... | collective-permute-start | bytes 245768 | tf_op jit(solution)/shard_map/ppermute | solution.py:444
  17.3 8.3 %collective-permute-start.7 = (f32[160,128]{1,0:T(8,128)S(1)}, f32[160,128]{1,0:T(8,128)S(1)}, u32[]{:S(2)}, u32[]{:S(2)}) collective-permute-start(f32[160,128]{1,0:T(8,128)S(1)} %get-tuple-element.38), channel_id=1, source_target_pairs={{1,2},{3,4},{5,6},{7,8},{9,10},{11,12},{13,14},{15,16},{17,18},{19... | collective-permute-start | bytes 245768 | tf_op jit(solution)/shard_map/ppermute | solution.py:444
where the time goes:
time: 26.5 us; the launch traced here: 26.4 us
  starting transfers between devices  18.5 us (70%)
  Pallas kernels  4.01 us (15%)
  waiting for transfers between devices  2.73 us (10%)
  local copies, waits for them, and re-layouts  1 us (4%)
    ppermute x8, starting transfers between devices, swap_with(): return lax.ppermute(value, axis, pairs + [(b, a) for a, b in pairs])  18.5 us
    ppermute x8, waiting for transfers between devices, swap_with(): return lax.ppermute(value, axis, pairs + [(b, a) for a, b in pairs])  2.73 us
    pallas_call x1, Pallas kernels, local(): pl.pallas_call(inner_kernel, out_shape=[jax.ShapeDtypeStruct((8,), jnp.in...  1.51 us
    pallas_call x1, Pallas kernels, local(): pl.pallas_call(outer_kernel, out_shape=[tiles_of(CELLS), tiles_of(PACKED)...  1.19 us
    unnamed x14, local copies, waits for them, and re-layouts  1 us
    pallas_call x1, Pallas kernels, local(): pl.pallas_call(place_kernel, out_shape=jax.ShapeDtypeStruct(out_shape, jn...  0.78 us
  transfers between devices with their start and end apart: 8, of which 1 were waited for; matrix products, arithmetic and copies ran while one was open for 0% of the time, Pallas kernels for 6%

commit v1 on v0

--- a/solution.py
+++ b/solution.py
@@ -16,7 +16,7 @@
 FACE_TILES = 12
 INNER = 9
 OUTER = 4
-FACE_CHUNK = 3
+FACE_CHUNK = 9
 PACKED = 2 * CELLS // SUB
 VMEM_LIMIT = 48 * 1024 * 1024
 
@@ -315,7 +315,7 @@
     copy = pltpu.make_async_copy(sent_info_ref, info_ref, sem)
     copy.start()
 
-    for face in range(6):
+    def fetch(face):
         axis, side = face // 2, face % 2
         from_row = index_ref[rows(3 * face), :]
         from_lane = index_ref[rows(3 * face + 1), :]
@@ -349,7 +349,7 @@
                 row = face * FACE_TILES + face_tile(ORDER[axis].index(f)) + k
                 ghost_ref[rows(row), :] = jnp.take_along_axis(chosen, after[0], axis=after[1])
 
-    for axis in range(3):
+    def edges(axis):
         for side in range(2):
             face = axis * 2 + side
 
@@ -382,14 +382,25 @@
         ]
         return [faces[k + 1] - faces[k] for k in range(EDGE)]
 
+    fetch(4)
+    fetch(5)
+    fetch(2)
+    fetch(3)
+    edges(2)
+    fetch(0)
+    fetch(1)
+    for f in range(FIELDS):
+        tiles = from_z(change(2, f), turn_ref.at[rows(f * EDGE, EDGE)])
+        turn_ref[rows(f * EDGE, EDGE), :] = jnp.concatenate(tiles, axis=0)
+    edges(1)
+    edges(0)
     scale = scale_ref[...]
     for f in range(FIELDS):
         along_x = change(0, f)
         along_y = swap_xy(change(1, f))
-        along_z = from_z(change(2, f), turn_ref.at[rows(f * EDGE, EDGE)])
         for x in range(EDGE):
-            total = along_x[x] + along_y[x] + along_z[x]
             place = rows(f * EDGE + x)
+            total = along_x[x] + along_y[x] + turn_ref[place, :]
             new_ref[place, :] = c_ref[place, :] - scale * total
     copy.wait()
     last = info_ref[0]

time: 26.5 us -> 26.5 us (level)
  no operation moved by 1% of the time
where the time goes in v1:
time: 26.5 us; the launch traced here: 26.4 us
  starting transfers between devices  18.5 us (70%)
  Pallas kernels  4 us (15%)
  waiting for transfers between devices  2.73 us (10%)
  local copies, waits for them, and re-layouts  1 us (4%)
    ppermute x8, starting transfers between devices, swap_with(): return lax.ppermute(value, axis, pairs + [(b, a) for a, b in pairs])  18.5 us
    ppermute x8, waiting for transfers between devices, swap_with(): return lax.ppermute(value, axis, pairs + [(b, a) for a, b in pairs])  2.73 us
    pallas_call x1, Pallas kernels, local(): pl.pallas_call(inner_kernel, out_shape=[jax.ShapeDtypeStruct((8,), jnp.in...  1.51 us
    pallas_call x1, Pallas kernels, local(): pl.pallas_call(outer_kernel, out_shape=[tiles_of(CELLS), tiles_of(PACKED)...  1.18 us
    unnamed x14, local copies, waits for them, and re-layouts  1 us
    pallas_call x1, Pallas kernels, local(): pl.pallas_call(place_kernel, out_shape=jax.ShapeDtypeStruct(out_shape, jn...  0.78 us
  transfers between devices with their start and end apart: 8, of which 1 were waited for; matrix products, arithmetic and copies ran while one was open for 0% of the time, Pallas kernels for 6%

profile of v1, /device:TPU:1, one launch (start us, length us, event | category | flops | bytes accessed | tf_op | source)
XLA Modules:
  0.0 26.4 jit_solution(14445749951707464454)
XLA Ops:
  0.0 0.0 copy-start
  0.0 1.0 %copy-done = f32[4,5,4096]{2,0,1:T(4,128)S(1)} copy-done((f32[4,5,4096]{2,0,1:T(4,128)S(1)}, f32[4,5,4096]{2,0,1:T(4,128)}, u32[]{:S(2)}) %copy-start) | copy-done | bytes 327704
  1.0 0.5 %layers.1 = (f32[96,128]{1,0:T(8,128)S(1)}, f32[96,128]{1,0:T(8,128)S(1)}, f32[96,128]{1,0:T(8,128)S(1)}, f32[96,128]{1,0:T(8,128)S(1)}, f32[96,128]{1,0:T(8,128...) custom-call(f32[640,128]{1,0:T(8,128)S(1)} %bitcast.8), custom_call_target="tpu_custom_call" | custom-call | tf_op jit(solution)/shard_map/layers/pallas_call | solution.py:473
  1.5 3.3 %collective-permute-start = (f32[96,128]{1,0:T(8,128)S(1)}, f32[96,128]{1,0:T(8,128)S(1)}, u32[]{:S(2)}, u32[]{:S(2)}) collective-permute-start(f32[96,128]{1,0:T(8,128)S(1)} %get-tuple-element.26), channel_id=1, source_target_pairs={{0,32},{64,96},{128,160},{192,224},{32,0},{96,64},{160,128},{224,1... | collective-permute-start | bytes 147464 | tf_op jit(solution)/shard_map/ppermute | solution.py:455
  4.8 0.0 copy-start.6
  4.8 0.0 collective-permute-start.1
  4.8 1.2 %collective-permute-start.2 = (f32[96,128]{1,0:T(8,128)S(1)}, f32[96,128]{1,0:T(8,128)S(1)}, u32[]{:S(2)}, u32[]{:S(2)}) collective-permute-start(f32[96,128]{1,0:T(8,128)S(1)} %get-tuple-element.28), channel_id=1, source_target_pairs={{0,1},{2,3},{4,5},{6,7},{1,0},{3,2},{5,4},{7,6},{8,9},{10,11},{12,... | collective-permute-start | bytes 147464 | tf_op jit(solution)/shard_map/ppermute | solution.py:455
  6.0 0.0 copy-start.4
  6.0 0.0 copy-start.5
  6.0 1.7 %collective-permute-start.3 = (f32[96,128]{1,0:T(8,128)S(1)}, f32[96,128]{1,0:T(8,128)S(1)}, u32[]{:S(2)}, u32[]{:S(2)}) collective-permute-start(f32[96,128]{1,0:T(8,128)S(1)} %get-tuple-element.29), channel_id=1, source_target_pairs={{32,64},{96,128},{160,192},{224,0},{64,32},{128,96},{192,160},{0,2... | collective-permute-start | bytes 147464 | tf_op jit(solution)/shard_map/ppermute | solution.py:455
  7.8 1.9 %collective-permute-start.4 = (f32[96,128]{1,0:T(8,128)S(1)}, f32[96,128]{1,0:T(8,128)S(1)}, u32[]{:S(2)}, u32[]{:S(2)}) collective-permute-start(f32[96,128]{1,0:T(8,128)S(1)} %get-tuple-element.30), channel_id=1, source_target_pairs={{8,16},{24,0},{16,8},{0,24},{9,17},{25,1},{17,9},{1,25},{10,18},{2... | collective-permute-start | bytes 147464 | tf_op jit(solution)/shard_map/ppermute | solution.py:455
  9.7 0.0 collective-permute-done.refs_2_
  9.7 0.0 copy-start.3
  9.7 0.0 copy-start.2
  9.7 4.7 %collective-permute-start.5 = (f32[96,128]{1,0:T(8,128)S(1)}, f32[96,128]{1,0:T(8,128)S(1)}, u32[]{:S(2)}, u32[]{:S(2)}) collective-permute-start(f32[96,128]{1,0:T(8,128)S(1)} %get-tuple-element.31), channel_id=1, source_target_pairs={{1,2},{3,4},{5,6},{7,0},{2,1},{4,3},{6,5},{0,7},{9,10},{11,12},{13... | collective-permute-start | bytes 147464 | tf_op jit(solution)/shard_map/ppermute | solution.py:455
  14.4 0.0 copy-done.6
  14.4 0.0 copy-done.4
  14.4 0.0 copy-done.5
  14.4 0.0 copy-done.3
  14.4 0.0 copy-done.2
  14.4 0.0 copy-start.1
  14.4 1.5 %inner.1 = (s32[8]{0:T(128)S(1)}, s32[160,128]{1,0:T(8,128)S(1)}, f32[8,128]{1,0:T(8,128)S(1)}, f32[640,128]{1,0:T(8,128)S(1)}, f32[1080,128]{1,0:T(8,128)S(1)}, /*index=5*/f32[240,128]{1,0:T(8,128)S(1)}) custom-call(s32[512]{0:T(512)S(1)} %copy-done.2, s32[512]{0:T(512)S(1)} %copy-done.3, s32[512]{0:T(512)S(1)} %copy-done.4, s32[4,6]{1,0:T(4,128)S(1)} %copy-done.5, ...), custom_call_target="tpu_custom_call" | custom-call | tf_op jit(solution)/shard_map/inner/pallas_call | solution.py:483
  15.9 0.0 collective-permute-done.1.refs_3_
  15.9 0.0 collective-permute-done.2.refs_4_
  15.9 0.0 collective-permute-done.3.refs_5_
  15.9 0.0 collective-permute-done.4.refs_6_
  16.0 0.0 collective-permute-done.5.refs_7_
  16.0 0.0 copy-done.1
  16.0 1.2 %outer.1 = (f32[640,128]{1,0:T(8,128)S(1)}, f32[160,128]{1,0:T(8,128)S(1)}, f32[160,128]{1,0:T(8,128)S(1)}) custom-call(s32[8]{0:T(128)S(1)} %get-tuple-element.25.refs_0_, f32[640,128]{1,0:T(8,128)S(1)} %bitcast.9, f32[96,128]{1,0:T(8,128)S(1)} %collective-permute-done.refs_2_, f32[96,128]{1,0:T(8,128)S(1)} %collective-permute-done.1.refs_3_, ...), custom_call_target="tpu_custom_call" | custom-call | tf_op jit(solution)/shard_map/outer/pallas_call | solution.py:501
  17.2 0.1 collective-permute-start.6
  17.3 5.6 %collective-permute-start.7 = (f32[160,128]{1,0:T(8,128)S(1)}, f32[160,128]{1,0:T(8,128)S(1)}, u32[]{:S(2)}, u32[]{:S(2)}) collective-permute-start(f32[160,128]{1,0:T(8,128)S(1)} %get-tuple-element.38), channel_id=1, source_target_pairs={{1,2},{3,4},{5,6},{7,8},{9,10},{11,12},{13,14},{15,16},{17,18},{19... | collective-permute-start | bytes 245768 | tf_op jit(solution)/shard_map/ppermute | solution.py:455
  22.9 0.0 collective-permute-done.6.near_ref
  22.9 2.7 %collective-permute-done.7.far_ref = f32[160,128]{1,0:T(8,128)S(1)} collective-permute-done((f32[160,128]{1,0:T(8,128)S(1)}, f32[160,128]{1,0:T(8,128)S(1)}, u32[]{:S(2)}, u32[]{:S(2)}) %collective-permute-start.7) | collective-permute-done | bytes 81952 | tf_op jit(solution)/shard_map/ppermute | solution.py:455
  25.6 0.8 %place.1 = f32[5,3,4096]{2,1,0:T(4,128)} custom-call(s32[160,128]{1,0:T(8,128)S(1)} %get-tuple-element.24.refs_10_.index_ref, f32[640,128]{1,0:T(8,128)S(1)} %settle.1.settled_ref, f32[160,128]{1,0:T(8,128)S(1)} %collective-permute-done.6.near_ref, f32[160,128]{1,0:T(8,128)S(1)} %collective-permute-done.7.far_ref), custom_call_target="tpu_custom_call" | custom-call | tf_op jit(solution)/shard_map/place/pallas_call | solution.py:535
  (1 shorter events, 0.0 us)
Async XLA Ops:
  0.0 1.0 %copy-start = (f32[4,5,4096]{2,0,1:T(4,128)S(1)}, f32[4,5,4096]{2,0,1:T(4,128)}, u32[]{:S(2)}) copy-start(f32[4,5,4096]{2,0,1:T(4,128)} %param.6) | copy-start | bytes 983044
  1.5 8.2 %collective-permute-start = (f32[96,128]{1,0:T(8,128)S(1)}, f32[96,128]{1,0:T(8,128)S(1)}, u32[]{:S(2)}, u32[]{:S(2)}) collective-permute-start(f32[96,128]{1,0:T(8,128)S(1)} %get-tuple-element.26), channel_id=1, source_target_pairs={{0,32},{64,96},{128,160},{192,224},{32,0},{96,64},{160,128},{224,1... | collective-permute-start | bytes 147464 | tf_op jit(solution)/shard_map/ppermute | solution.py:455
  4.8 9.6 %copy-start.6 = (s32[4,6]{1,0:T(4,128)S(1)}, s32[4,6]{1,0:T(4,128)}, u32[]{:S(2)}) copy-start(s32[4,6]{1,0:T(4,128)} %refs_4_.1) | copy-start | bytes 292
  4.8 11.1 %collective-permute-start.1 = (f32[96,128]{1,0:T(8,128)S(1)}, f32[96,128]{1,0:T(8,128)S(1)}, u32[]{:S(2)}, u32[]{:S(2)}) collective-permute-start(f32[96,128]{1,0:T(8,128)S(1)} %get-tuple-element.27), channel_id=1, source_target_pairs={{0,8},{16,24},{8,0},{24,16},{1,9},{17,25},{9,1},{25,17},{2,10},{18... | collective-permute-start | bytes 147464 | tf_op jit(solution)/shard_map/ppermute | solution.py:455
  4.8 11.1 %collective-permute-start.2 = (f32[96,128]{1,0:T(8,128)S(1)}, f32[96,128]{1,0:T(8,128)S(1)}, u32[]{:S(2)}, u32[]{:S(2)}) collective-permute-start(f32[96,128]{1,0:T(8,128)S(1)} %get-tuple-element.28), channel_id=1, source_target_pairs={{0,1},{2,3},{4,5},{6,7},{1,0},{3,2},{5,4},{7,6},{8,9},{10,11},{12,... | collective-permute-start | bytes 147464 | tf_op jit(solution)/shard_map/ppermute | solution.py:455
  6.0 8.3 %copy-start.4 = (s32[512]{0:T(512)S(1)}, s32[512]{0:T(512)}, u32[]{:S(2)}) copy-start(s32[512]{0:T(512)} %refs_2_.1) | copy-start | bytes 6148
  6.0 8.3 %copy-start.5 = (s32[4,6]{1,0:T(4,128)S(1)}, s32[4,6]{1,0:T(4,128)}, u32[]{:S(2)}) copy-start(s32[4,6]{1,0:T(4,128)} %refs_3_.1) | copy-start | bytes 292
  6.0 9.9 %collective-permute-start.3 = (f32[96,128]{1,0:T(8,128)S(1)}, f32[96,128]{1,0:T(8,128)S(1)}, u32[]{:S(2)}, u32[]{:S(2)}) collective-permute-start(f32[96,128]{1,0:T(8,128)S(1)} %get-tuple-element.29), channel_id=1, source_target_pairs={{32,64},{96,128},{160,192},{224,0},{64,32},{128,96},{192,160},{0,2... | collective-permute-start | bytes 147464 | tf_op jit(solution)/shard_map/ppermute | solution.py:455
  7.8 8.2 %collective-permute-start.4 = (f32[96,128]{1,0:T(8,128)S(1)}, f32[96,128]{1,0:T(8,128)S(1)}, u32[]{:S(2)}, u32[]{:S(2)}) collective-permute-start(f32[96,128]{1,0:T(8,128)S(1)} %get-tuple-element.30), channel_id=1, source_target_pairs={{8,16},{24,0},{16,8},{0,24},{9,17},{25,1},{17,9},{1,25},{10,18},{2... | collective-permute-start | bytes 147464 | tf_op jit(solution)/shard_map/ppermute | solution.py:455
  9.7 4.7 %copy-start.3 = (s32[512]{0:T(512)S(1)}, s32[512]{0:T(512)}, u32[]{:S(2)}) copy-start(s32[512]{0:T(512)} %refs_1_.1) | copy-start | bytes 6148
  9.7 4.7 %copy-start.2 = (s32[512]{0:T(512)S(1)}, s32[512]{0:T(512)}, u32[]{:S(2)}) copy-start(s32[512]{0:T(512)} %refs_0_.1) | copy-start | bytes 6148
  9.7 6.3 %collective-permute-start.5 = (f32[96,128]{1,0:T(8,128)S(1)}, f32[96,128]{1,0:T(8,128)S(1)}, u32[]{:S(2)}, u32[]{:S(2)}) collective-permute-start(f32[96,128]{1,0:T(8,128)S(1)} %get-tuple-element.31), channel_id=1, source_target_pairs={{1,2},{3,4},{5,6},{7,0},{2,1},{4,3},{6,5},{0,7},{9,10},{11,12},{13... | collective-permute-start | bytes 147464 | tf_op jit(solution)/shard_map/ppermute | solution.py:455
  14.4 1.6 %copy-start.1 = (f32[4,5,4096]{2,0,1:T(4,128)S(1)}, f32[4,5,4096]{2,0,1:T(4,128)}, u32[]{:S(2)}) copy-start(f32[4,5,4096]{2,0,1:T(4,128)} %param.6) | copy-start | bytes 983044
  17.2 5.7 %collective-permute-start.6 = (f32[160,128]{1,0:T(8,128)S(1)}, f32[160,128]{1,0:T(8,128)S(1)}, u32[]{:S(2)}, u32[]{:S(2)}) collective-permute-start(f32[160,128]{1,0:T(8,128)S(1)} %get-tuple-element.37), channel_id=1, source_target_pairs={{0,1},{2,3},{4,5},{6,7},{8,9},{10,11},{12,13},{14,15},{16,17},{18,... | collective-permute-start | bytes 245768 | tf_op jit(solution)/shard_map/ppermute | solution.py:455
  17.3 8.3 %collective-permute-start.7 = (f32[160,128]{1,0:T(8,128)S(1)}, f32[160,128]{1,0:T(8,128)S(1)}, u32[]{:S(2)}, u32[]{:S(2)}) collective-permute-start(f32[160,128]{1,0:T(8,128)S(1)} %get-tuple-element.38), channel_id=1, source_target_pairs={{1,2},{3,4},{5,6},{7,8},{9,10},{11,12},{13,14},{15,16},{17,18},{19... | collective-permute-start | bytes 245768 | tf_op jit(solution)/shard_map/ppermute | solution.py:455

commit v2 on v1

--- a/solution.py
+++ b/solution.py
@@ -307,7 +307,7 @@
 
 def outer_kernel(*refs):
     sent_info_ref, c_ref = refs[0:2]
-    near_got, far_got = refs[2:5], refs[5:8]
+    near_got, far_got = (refs[2], refs[4], refs[3]), refs[5:8]
     w_ref, z_ref, index_ref, scale_ref, y_ref, inner_ref, edge_ref = refs[8:15]
     new_ref, near_ref, far_ref = refs[15:18]
     ghost_ref, flux_ref, turn_ref, info_ref, sem = refs[18:23]
@@ -515,7 +515,7 @@
     )(
         info,
         cells,
-        *got,
+        *(got[k] for k in (0, 2, 1, 3, 4, 5)),
         along_x,
         along_z,
         index,

time: 26.5 us -> 26.5 us (level)
  no operation moved by 1% of the time
where the time goes in v2:
time: 26.5 us; the launch traced here: 26.3 us
  starting transfers between devices  18.5 us (70%)
  Pallas kernels  4 us (15%)
  waiting for transfers between devices  2.73 us (10%)
  local copies, waits for them, and re-layouts  1 us (4%)
    ppermute x8, starting transfers between devices, swap_with(): return lax.ppermute(value, axis, pairs + [(b, a) for a, b in pairs])  18.5 us
    ppermute x8, waiting for transfers between devices, swap_with(): return lax.ppermute(value, axis, pairs + [(b, a) for a, b in pairs])  2.73 us
    pallas_call x1, Pallas kernels, local(): pl.pallas_call(inner_kernel, out_shape=[jax.ShapeDtypeStruct((8,), jnp.in...  1.51 us
    pallas_call x1, Pallas kernels, local(): pl.pallas_call(outer_kernel, out_shape=[tiles_of(CELLS), tiles_of(PACKED)...  1.17 us
    unnamed x14, local copies, waits for them, and re-layouts  1 us
    pallas_call x1, Pallas kernels, local(): pl.pallas_call(place_kernel, out_shape=jax.ShapeDtypeStruct(out_shape, jn...  0.78 us
  transfers between devices with their start and end apart: 8, of which 1 were waited for; matrix products, arithmetic and copies ran while one was open for 0% of the time, Pallas kernels for 6%

profile of v2, /device:TPU:1, one launch (start us, length us, event | category | flops | bytes accessed | tf_op | source)
XLA Modules:
  0.0 26.3 jit_solution(16233690727282490970)
XLA Ops:
  0.0 0.0 copy-start
  0.0 1.0 %copy-done = f32[4,5,4096]{2,0,1:T(4,128)S(1)} copy-done((f32[4,5,4096]{2,0,1:T(4,128)S(1)}, f32[4,5,4096]{2,0,1:T(4,128)}, u32[]{:S(2)}) %copy-start) | copy-done | bytes 327704
  1.0 0.5 %layers.1 = (f32[96,128]{1,0:T(8,128)S(1)}, f32[96,128]{1,0:T(8,128)S(1)}, f32[96,128]{1,0:T(8,128)S(1)}, f32[96,128]{1,0:T(8,128)S(1)}, f32[96,128]{1,0:T(8,128...) custom-call(f32[640,128]{1,0:T(8,128)S(1)} %bitcast.8), custom_call_target="tpu_custom_call" | custom-call | tf_op jit(solution)/shard_map/layers/pallas_call | solution.py:473
  1.5 3.3 %collective-permute-start = (f32[96,128]{1,0:T(8,128)S(1)}, f32[96,128]{1,0:T(8,128)S(1)}, u32[]{:S(2)}, u32[]{:S(2)}) collective-permute-start(f32[96,128]{1,0:T(8,128)S(1)} %get-tuple-element.26), channel_id=1, source_target_pairs={{0,32},{64,96},{128,160},{192,224},{32,0},{96,64},{160,128},{224,1... | collective-permute-start | bytes 147464 | tf_op jit(solution)/shard_map/ppermute | solution.py:455
  4.8 0.0 copy-start.6
  4.8 0.0 collective-permute-start.1
  4.8 1.2 %collective-permute-start.2 = (f32[96,128]{1,0:T(8,128)S(1)}, f32[96,128]{1,0:T(8,128)S(1)}, u32[]{:S(2)}, u32[]{:S(2)}) collective-permute-start(f32[96,128]{1,0:T(8,128)S(1)} %get-tuple-element.28), channel_id=1, source_target_pairs={{0,8},{16,24},{8,0},{24,16},{1,9},{17,25},{9,1},{25,17},{2,10},{18... | collective-permute-start | bytes 147464 | tf_op jit(solution)/shard_map/ppermute | solution.py:455
  6.0 0.0 copy-start.4
  6.0 0.0 copy-start.5
  6.0 1.7 %collective-permute-start.3 = (f32[96,128]{1,0:T(8,128)S(1)}, f32[96,128]{1,0:T(8,128)S(1)}, u32[]{:S(2)}, u32[]{:S(2)}) collective-permute-start(f32[96,128]{1,0:T(8,128)S(1)} %get-tuple-element.29), channel_id=1, source_target_pairs={{32,64},{96,128},{160,192},{224,0},{64,32},{128,96},{192,160},{0,2... | collective-permute-start | bytes 147464 | tf_op jit(solution)/shard_map/ppermute | solution.py:455
  7.8 1.9 %collective-permute-start.4 = (f32[96,128]{1,0:T(8,128)S(1)}, f32[96,128]{1,0:T(8,128)S(1)}, u32[]{:S(2)}, u32[]{:S(2)}) collective-permute-start(f32[96,128]{1,0:T(8,128)S(1)} %get-tuple-element.30), channel_id=1, source_target_pairs={{8,16},{24,0},{16,8},{0,24},{9,17},{25,1},{17,9},{1,25},{10,18},{2... | collective-permute-start | bytes 147464 | tf_op jit(solution)/shard_map/ppermute | solution.py:455
  9.7 0.0 collective-permute-done.refs_2_
  9.7 0.0 copy-start.3
  9.7 0.0 copy-start.2
  9.7 4.7 %collective-permute-start.5 = (f32[96,128]{1,0:T(8,128)S(1)}, f32[96,128]{1,0:T(8,128)S(1)}, u32[]{:S(2)}, u32[]{:S(2)}) collective-permute-start(f32[96,128]{1,0:T(8,128)S(1)} %get-tuple-element.31), channel_id=1, source_target_pairs={{1,2},{3,4},{5,6},{7,0},{2,1},{4,3},{6,5},{0,7},{9,10},{11,12},{13... | collective-permute-start | bytes 147464 | tf_op jit(solution)/shard_map/ppermute | solution.py:455
  14.4 0.0 copy-done.6
  14.4 0.0 copy-done.4
  14.4 0.0 copy-done.5
  14.4 0.0 copy-done.3
  14.4 0.0 copy-done.2
  14.4 0.0 copy-start.1
  14.4 1.5 %inner.1 = (s32[8]{0:T(128)S(1)}, s32[160,128]{1,0:T(8,128)S(1)}, f32[8,128]{1,0:T(8,128)S(1)}, f32[640,128]{1,0:T(8,128)S(1)}, f32[1080,128]{1,0:T(8,128)S(1)}, /*index=5*/f32[240,128]{1,0:T(8,128)S(1)}) custom-call(s32[512]{0:T(512)S(1)} %copy-done.2, s32[512]{0:T(512)S(1)} %copy-done.3, s32[512]{0:T(512)S(1)} %copy-done.4, s32[4,6]{1,0:T(4,128)S(1)} %copy-done.5, ...), custom_call_target="tpu_custom_call" | custom-call | tf_op jit(solution)/shard_map/inner/pallas_call | solution.py:483
  15.9 0.0 collective-permute-done.1.refs_3_
  15.9 0.0 collective-permute-done.2.refs_4_
  15.9 0.0 collective-permute-done.3.refs_5_
  15.9 0.0 collective-permute-done.4.refs_6_
  16.0 0.0 collective-permute-done.5.refs_7_
  16.0 0.0 copy-done.1
  16.0 1.2 %outer.1 = (f32[640,128]{1,0:T(8,128)S(1)}, f32[160,128]{1,0:T(8,128)S(1)}, f32[160,128]{1,0:T(8,128)S(1)}) custom-call(s32[8]{0:T(128)S(1)} %get-tuple-element.25.refs_0_, f32[640,128]{1,0:T(8,128)S(1)} %bitcast.9, f32[96,128]{1,0:T(8,128)S(1)} %collective-permute-done.refs_2_, f32[96,128]{1,0:T(8,128)S(1)} %collective-permute-done.1.refs_3_, ...), custom_call_target="tpu_custom_call" | custom-call | tf_op jit(solution)/shard_map/outer/pallas_call | solution.py:501
  17.2 0.1 collective-permute-start.6
  17.3 5.6 %collective-permute-start.7 = (f32[160,128]{1,0:T(8,128)S(1)}, f32[160,128]{1,0:T(8,128)S(1)}, u32[]{:S(2)}, u32[]{:S(2)}) collective-permute-start(f32[160,128]{1,0:T(8,128)S(1)} %get-tuple-element.38), channel_id=1, source_target_pairs={{1,2},{3,4},{5,6},{7,8},{9,10},{11,12},{13,14},{15,16},{17,18},{19... | collective-permute-start | bytes 245768 | tf_op jit(solution)/shard_map/ppermute | solution.py:455
  22.8 0.0 collective-permute-done.6.near_ref
  22.9 2.7 %collective-permute-done.7.far_ref = f32[160,128]{1,0:T(8,128)S(1)} collective-permute-done((f32[160,128]{1,0:T(8,128)S(1)}, f32[160,128]{1,0:T(8,128)S(1)}, u32[]{:S(2)}, u32[]{:S(2)}) %collective-permute-start.7) | collective-permute-done | bytes 81952 | tf_op jit(solution)/shard_map/ppermute | solution.py:455
  25.6 0.8 %place.1 = f32[5,3,4096]{2,1,0:T(4,128)} custom-call(s32[160,128]{1,0:T(8,128)S(1)} %get-tuple-element.24.refs_10_.index_ref, f32[640,128]{1,0:T(8,128)S(1)} %settle.1.settled_ref, f32[160,128]{1,0:T(8,128)S(1)} %collective-permute-done.6.near_ref, f32[160,128]{1,0:T(8,128)S(1)} %collective-permute-done.7.far_ref), custom_call_target="tpu_custom_call" | custom-call | tf_op jit(solution)/shard_map/place/pallas_call | solution.py:535
  (1 shorter events, 0.0 us)
Async XLA Ops:
  0.0 1.0 %copy-start = (f32[4,5,4096]{2,0,1:T(4,128)S(1)}, f32[4,5,4096]{2,0,1:T(4,128)}, u32[]{:S(2)}) copy-start(f32[4,5,4096]{2,0,1:T(4,128)} %param.6) | copy-start | bytes 983044
  1.5 8.2 %collective-permute-start = (f32[96,128]{1,0:T(8,128)S(1)}, f32[96,128]{1,0:T(8,128)S(1)}, u32[]{:S(2)}, u32[]{:S(2)}) collective-permute-start(f32[96,128]{1,0:T(8,128)S(1)} %get-tuple-element.26), channel_id=1, source_target_pairs={{0,32},{64,96},{128,160},{192,224},{32,0},{96,64},{160,128},{224,1... | collective-permute-start | bytes 147464 | tf_op jit(solution)/shard_map/ppermute | solution.py:455
  4.8 9.6 %copy-start.6 = (s32[4,6]{1,0:T(4,128)S(1)}, s32[4,6]{1,0:T(4,128)}, u32[]{:S(2)}) copy-start(s32[4,6]{1,0:T(4,128)} %refs_4_.1) | copy-start | bytes 292
  4.8 11.1 %collective-permute-start.1 = (f32[96,128]{1,0:T(8,128)S(1)}, f32[96,128]{1,0:T(8,128)S(1)}, u32[]{:S(2)}, u32[]{:S(2)}) collective-permute-start(f32[96,128]{1,0:T(8,128)S(1)} %get-tuple-element.27), channel_id=1, source_target_pairs={{0,1},{2,3},{4,5},{6,7},{1,0},{3,2},{5,4},{7,6},{8,9},{10,11},{12,... | collective-permute-start | bytes 147464 | tf_op jit(solution)/shard_map/ppermute | solution.py:455
  4.8 11.1 %collective-permute-start.2 = (f32[96,128]{1,0:T(8,128)S(1)}, f32[96,128]{1,0:T(8,128)S(1)}, u32[]{:S(2)}, u32[]{:S(2)}) collective-permute-start(f32[96,128]{1,0:T(8,128)S(1)} %get-tuple-element.28), channel_id=1, source_target_pairs={{0,8},{16,24},{8,0},{24,16},{1,9},{17,25},{9,1},{25,17},{2,10},{18... | collective-permute-start | bytes 147464 | tf_op jit(solution)/shard_map/ppermute | solution.py:455
  6.0 8.3 %copy-start.4 = (s32[512]{0:T(512)S(1)}, s32[512]{0:T(512)}, u32[]{:S(2)}) copy-start(s32[512]{0:T(512)} %refs_2_.1) | copy-start | bytes 6148
  6.0 8.3 %copy-start.5 = (s32[4,6]{1,0:T(4,128)S(1)}, s32[4,6]{1,0:T(4,128)}, u32[]{:S(2)}) copy-start(s32[4,6]{1,0:T(4,128)} %refs_3_.1) | copy-start | bytes 292
  6.0 9.9 %collective-permute-start.3 = (f32[96,128]{1,0:T(8,128)S(1)}, f32[96,128]{1,0:T(8,128)S(1)}, u32[]{:S(2)}, u32[]{:S(2)}) collective-permute-start(f32[96,128]{1,0:T(8,128)S(1)} %get-tuple-element.29), channel_id=1, source_target_pairs={{32,64},{96,128},{160,192},{224,0},{64,32},{128,96},{192,160},{0,2... | collective-permute-start | bytes 147464 | tf_op jit(solution)/shard_map/ppermute | solution.py:455
  7.8 8.2 %collective-permute-start.4 = (f32[96,128]{1,0:T(8,128)S(1)}, f32[96,128]{1,0:T(8,128)S(1)}, u32[]{:S(2)}, u32[]{:S(2)}) collective-permute-start(f32[96,128]{1,0:T(8,128)S(1)} %get-tuple-element.30), channel_id=1, source_target_pairs={{8,16},{24,0},{16,8},{0,24},{9,17},{25,1},{17,9},{1,25},{10,18},{2... | collective-permute-start | bytes 147464 | tf_op jit(solution)/shard_map/ppermute | solution.py:455
  9.7 4.7 %copy-start.3 = (s32[512]{0:T(512)S(1)}, s32[512]{0:T(512)}, u32[]{:S(2)}) copy-start(s32[512]{0:T(512)} %refs_1_.1) | copy-start | bytes 6148
  9.7 4.7 %copy-start.2 = (s32[512]{0:T(512)S(1)}, s32[512]{0:T(512)}, u32[]{:S(2)}) copy-start(s32[512]{0:T(512)} %refs_0_.1) | copy-start | bytes 6148
  9.7 6.3 %collective-permute-start.5 = (f32[96,128]{1,0:T(8,128)S(1)}, f32[96,128]{1,0:T(8,128)S(1)}, u32[]{:S(2)}, u32[]{:S(2)}) collective-permute-start(f32[96,128]{1,0:T(8,128)S(1)} %get-tuple-element.31), channel_id=1, source_target_pairs={{1,2},{3,4},{5,6},{7,0},{2,1},{4,3},{6,5},{0,7},{9,10},{11,12},{13... | collective-permute-start | bytes 147464 | tf_op jit(solution)/shard_map/ppermute | solution.py:455
  14.4 1.6 %copy-start.1 = (f32[4,5,4096]{2,0,1:T(4,128)S(1)}, f32[4,5,4096]{2,0,1:T(4,128)}, u32[]{:S(2)}) copy-start(f32[4,5,4096]{2,0,1:T(4,128)} %param.6) | copy-start | bytes 983044
  17.2 5.7 %collective-permute-start.6 = (f32[160,128]{1,0:T(8,128)S(1)}, f32[160,128]{1,0:T(8,128)S(1)}, u32[]{:S(2)}, u32[]{:S(2)}) collective-permute-start(f32[160,128]{1,0:T(8,128)S(1)} %get-tuple-element.37), channel_id=1, source_target_pairs={{0,1},{2,3},{4,5},{6,7},{8,9},{10,11},{12,13},{14,15},{16,17},{18,... | collective-permute-start | bytes 245768 | tf_op jit(solution)/shard_map/ppermute | solution.py:455
  17.3 8.3 %collective-permute-start.7 = (f32[160,128]{1,0:T(8,128)S(1)}, f32[160,128]{1,0:T(8,128)S(1)}, u32[]{:S(2)}, u32[]{:S(2)}) collective-permute-start(f32[160,128]{1,0:T(8,128)S(1)} %get-tuple-element.38), channel_id=1, source_target_pairs={{1,2},{3,4},{5,6},{7,8},{9,10},{11,12},{13,14},{15,16},{17,18},{19... | collective-permute-start | bytes 245768 | tf_op jit(solution)/shard_map/ppermute | solution.py:455
